TPU v7x, 32 devices: a whole 2x2x4 slice. The times are simulated.
32 devices in a mesh: wide: 32 (over z, y, x, core), narrow: 1.
Axes of the slice: x: 2, y: 2, z: 4, core: 2. Of those that a mesh axis runs over, the one named last changes fastest.
Arguments:
- field: float32 [256, 44, 512], P('wide', 'narrow')
- sketch_one: float32 [512, 128], replicated, may hold values from -6 to 6
- sketch_two: float32 [256, 128], replicated, may hold values from -6 to 6
- ranks: int32 [2], replicated, may hold values from 64 to 128, as said below
Outputs:
- core: float32 [128, 44, 128], P('wide', 'narrow')
Inputs may be any that keep to these rules, and one draw needn't show every extreme that they name: One of the two ranks equals 128.
All inputs are finite; a program needn't handle non-finite values.
Results may differ from a plain program's by a relative error of at most 0.00022.
Values sent between devices are 32-bit elements; how exact they have to be, the bound alone decides.
A program may use at most 64 MiB of HBM per device.

v0:
```python
import functools

import jax
import jax.numpy as jnp
from jax import lax
from jax.experimental import pallas as pl
from jax.experimental.pallas import tpu as pltpu
from jax.sharding import PartitionSpec as P

HIGHEST = lax.Precision.HIGHEST
MESH = pl.DeviceIdType.MESH


def make_basis(local, sketch, rank):
    keep = (jnp.arange(sketch.shape[1]) < rank).astype(jnp.float32)
    masked = sketch * keep
    part = jnp.einsum("akn,ns->aks", local, masked, precision=HIGHEST)
    part = jnp.einsum("akn,aks->ns", local, part, precision=HIGHEST)
    sketched = lax.psum(part, ("wide", "narrow"))
    inner = jnp.dot(sketched.T, sketched, precision=HIGHEST) + jnp.diag(1.0 - keep)
    lower = jnp.linalg.cholesky(inner)
    return jax.scipy.linalg.solve_triangular(lower, sketched.T, lower=True)


def general(field, sketch_one, sketch_two, ranks):
    basis_one = make_basis(field, sketch_one, ranks[0])
    core_one = jnp.einsum("rn,ykn->rky", basis_one, field, precision=HIGHEST)
    regrouped = lax.all_to_all(core_one, "wide", split_axis=0, concat_axis=2, tiled=True)
    basis_two = make_basis(regrouped, sketch_two, ranks[1])
    return jnp.einsum("sn,rkn->rks", basis_two, regrouped, precision=HIGHEST)


def dot(a, b, dims):
    return lax.dot_general(
        a, b, (dims, ((), ())), precision=HIGHEST, preferred_element_type=jnp.float32
    )


NN = ((1,), (0,))
NT = ((1,), (1,))
TN = ((0,), (0,))
BLOCK = 8
TILES = 4


def inverse_factor(work, linv):
    size = linv.shape[0]
    tile = (BLOCK, size)
    group = TILES * BLOCK
    sub = lax.broadcasted_iota(jnp.int32, tile, 0)

    for r0 in range(0, size, group):
        own = work[r0 : r0 + group, :size]
        rest = work[r0 : r0 + group, size:]
        rows_a = [own[u * BLOCK : (u + 1) * BLOCK, :] for u in range(TILES)]
        rows_t = [rest[u * BLOCK : (u + 1) * BLOCK, :] for u in range(TILES)]
        panels_a, panels_t = [], []
        for u in range(TILES):
            d, below = {}, {}
            for q in range(BLOCK):
                lane = r0 + u * BLOCK + q
                column = jnp.broadcast_to(rows_a[u][:, lane : lane + 1], tile)
                for p in range(q, BLOCK):
                    d[p, q] = jnp.broadcast_to(column[p : p + 1, :], tile)
                for v in range(u + 1, TILES):
                    below[v, q] = jnp.broadcast_to(rows_a[v][:, lane : lane + 1], tile)
            done_a, done_t = [], []
            panel_a = jnp.zeros(tile, jnp.float32)
            panel_t = jnp.zeros(tile, jnp.float32)
            for j in range(BLOCK):
                x = d[j, j]
                y = lax.rsqrt(x)
                y = y * (1.5 - 0.5 * ((x * y) * y))
                for p in range(j + 1, BLOCK):
                    d[p, j] = d[p, j] * y
                for v in range(u + 1, TILES):
                    below[v, j] = below[v, j] * y
                for q in range(j + 1, BLOCK):
                    for p in range(q, BLOCK):
                        d[p, q] = d[p, q] - d[p, j] * d[q, j]
                    for v in range(u + 1, TILES):
                        below[v, q] = below[v, q] - below[v, j] * d[q, j]
                ra = jnp.broadcast_to(rows_a[u][j : j + 1, :], tile)
                rt = jnp.broadcast_to(rows_t[u][j : j + 1, :], tile)
                for k in range(j):
                    ra = ra - d[j, k] * done_a[k]
                    rt = rt - d[j, k] * done_t[k]
                ra = ra * y
                rt = rt * y
                done_a.append(ra)
                done_t.append(rt)
                panel_a = jnp.where(sub == j, ra, panel_a)
                panel_t = jnp.where(sub == j, rt, panel_t)
                for v in range(u + 1, TILES):
                    rows_a[v] = rows_a[v] - below[v, j] * ra
                    rows_t[v] = rows_t[v] - below[v, j] * rt
            panels_a.append(panel_a)
            panels_t.append(panel_t)
        panel_t = jnp.concatenate(panels_t, axis=0)
        panel_a = jnp.concatenate(panels_a, axis=0)
        linv[r0 : r0 + group, :] = panel_t
        end = r0 + group
        if end < size:
            both = jnp.concatenate([panel_a, panel_t], axis=1)
            work[end:, :] = work[end:, :] - dot(panel_a.T[end:, :], both, NN)


def fill_work(work, inner, keep_row, size):
    row = lax.broadcasted_iota(jnp.int32, (size, size), 0)
    col = lax.broadcasted_iota(jnp.int32, (size, size), 1)
    eye = (row == col).astype(jnp.float32)
    work[:, :size] = inner + eye * (1.0 - keep_row)
    work[:, size:] = eye


def kernel(
    n, field, sketch_one, sketch_two, ranks, out,
    flat, part_one, pair_one, got_one, full_one, work, linv, core, give, have,
    part_two, pair_two, got_two, full_two, send_sem, recv_sem,
):
    me = lax.axis_index("wide")
    ydev, kdim, n1 = field.shape
    size = sketch_one.shape[1]
    n2 = sketch_two.shape[0]
    stride = flat.shape[0] // ydev
    per = size // n

    barrier = pltpu.get_barrier_semaphore()

    def greet(i, carry):
        peer = lax.rem(me + 1 + i, n)
        pl.semaphore_signal(barrier, inc=1, device_id={"wide": peer}, device_id_type=MESH)
        return carry

    lax.fori_loop(0, n - 1, greet, 0)

    core_id = lax.rem(me, 2)
    chip = me // 2
    chips = n // 2

    def every(i):
        return lax.rem(me + 1 + i, n)

    def alike(i):
        return 2 * lax.rem(chip + 1 + i, chips) + core_id

    def twin(i):
        return chip * 2 + 1 - core_id

    def exchange(phase, count, peer_of, source, target, whole):
        def start(i, carry):
            peer = peer_of(i)
            pltpu.make_async_remote_copy(
                src_ref=source(peer), dst_ref=target(i),
                send_sem=send_sem.at[phase], recv_sem=recv_sem.at[phase],
                device_id={"wide": peer}, device_id_type=MESH,
            ).start()
            return carry

        lax.fori_loop(0, count, start, 0)
        everything = pltpu.make_async_remote_copy(
            src_ref=whole, dst_ref=whole,
            send_sem=send_sem.at[phase], recv_sem=recv_sem.at[phase],
            device_id={"wide": peer_of(0)}, device_id_type=MESH,
        )
        everything.wait_recv()
        everything.wait_send()

    def sum_over_devices(phase, part, pair, got, full, direct):
        rows = part.shape[0]
        half = rows // 2
        chunk = rows // n

        def half_of(device):
            return pl.ds(pl.multiple_of(lax.rem(device, 2) * half, 8), half)

        def chunk_of(device):
            start = lax.rem(device, 2) * half + (device // 2) * chunk
            return pl.ds(pl.multiple_of(start, 8), chunk)

        exchange(phase, 1, twin, lambda p: part.at[half_of(p), :], lambda i: pair, pair)
        mine = half_of(me)
        part[mine, :] = part[mine, :] + pair[...]
        exchange(
            phase + 1, chips - 1, alike,
            lambda p: part.at[chunk_of(p), :], lambda i: got.at[i], got,
        )
        own = chunk_of(me)
        full[own, :] = jnp.sum(got[...], axis=0) + part[own, :]
        if direct:
            exchange(
                phase + 2, n - 1, every,
                lambda p: full.at[own, :], lambda i: full.at[own, :],
                full.at[pl.ds(0, rows - chunk), :],
            )
            return
        exchange(
            phase + 2, chips - 1, alike,
            lambda p: full.at[own, :], lambda i: full.at[own, :],
            full.at[pl.ds(0, half - chunk), :],
        )
        exchange(
            phase + 3, 1, twin,
            lambda p: full.at[mine, :], lambda i: full.at[mine, :],
            full.at[pl.ds(0, half), :],
        )

    lane = lax.broadcasted_iota(jnp.int32, (1, size), 1)
    keep_one = (lane < ranks[0]).astype(jnp.float32)
    keep_two = (lane < ranks[1]).astype(jnp.float32)

    for y in range(ydev):
        flat[y * stride : y * stride + kdim, :] = field[y]
        flat[y * stride + kdim : (y + 1) * stride, :] = jnp.zeros(
            (stride - kdim, n1), jnp.float32
        )
    projected = dot(flat[...], sketch_one[...] * keep_one, NN)
    part_one[...] = dot(projected, flat[...], TN).T
    masked_two = (sketch_two[...] * keep_two).T

    pl.semaphore_wait(barrier, n - 1)

    sum_over_devices(0, part_one, pair_one, got_one, full_one, False)
    sk = full_one[...]
    fill_work(work, dot(sk, sk, TN), keep_one, size)
    rotated = dot(flat[...], sk, NN)
    inverse_factor(work, linv)
    mixed = dot(linv[...], rotated, NT)
    for t in range(ydev // 2):
        core[t] = mixed[:, 2 * stride * t : 2 * stride * (t + 1)]

    low = lax.broadcasted_iota(jnp.int32, (n, 2 * stride), 1) < stride
    for half in range(per // 2):
        for t in range(ydev // 2):
            first = core[t, pl.ds(2 * half, n, stride=per), :]
            second = core[t, pl.ds(2 * half + 1, n, stride=per), :]
            even = jnp.where(low, first, pltpu.roll(second, stride, 1))
            odd = jnp.where(low, pltpu.roll(first, stride, 1), second)
            give[half, pl.ds(2 * t, n, stride=ydev), :] = even
            give[half, pl.ds(2 * t + 1, n, stride=ydev), :] = odd
    mine_y = pl.ds(pl.multiple_of(me * ydev, ydev), ydev)
    have[:, mine_y, :] = give[:, mine_y, :]
    exchange(
        8, n - 1, every,
        lambda p: give.at[:, pl.ds(pl.multiple_of(p * ydev, ydev), ydev), :],
        lambda i: have.at[:, mine_y, :],
        have.at[:, pl.ds(0, n2 - ydev), :],
    )

    total = jnp.zeros((n2, size), jnp.float32)
    for half in range(per // 2):
        fibers = have[half]
        total = total + dot(fibers, dot(masked_two, fibers, NN), NT)
    part_two[...] = total
    sum_over_devices(4, part_two, pair_two, got_two, full_two, True)
    sk = full_two[...]
    fill_work(work, dot(sk, sk, TN), keep_two, size)
    spun = [dot(have[half], sk, TN) for half in range(per // 2)]
    inverse_factor(work, linv)
    for half in range(per // 2):
        done = dot(spun[half], linv[...], NT)
        for i in range(2):
            out[2 * half + i] = done[stride * i : stride * i + kdim, :]


def fused(n, field, sketch_one, sketch_two, ranks):
    ydev, kdim, n1 = field.shape
    n2, size = sketch_two.shape
    stride = size // 2
    vmem = pl.BlockSpec(memory_space=pltpu.VMEM)
    f32 = jnp.float32
    return pl.pallas_call(
        functools.partial(kernel, n),
        out_shape=jax.ShapeDtypeStruct((size // n, kdim, size), f32),
        in_specs=[vmem, vmem, vmem, pl.BlockSpec(memory_space=pltpu.SMEM)],
        out_specs=vmem,
        scratch_shapes=[
            pltpu.VMEM((ydev * stride, n1), f32),
            pltpu.VMEM((n1, size), f32),
            pltpu.VMEM((n1 // 2, size), f32),
            pltpu.VMEM((n // 2 - 1, n1 // n, size), f32),
            pltpu.VMEM((n1, size), f32),
            pltpu.VMEM((size, 2 * size), f32),
            pltpu.VMEM((size, size), f32),
            pltpu.VMEM((ydev // 2, size, 2 * stride), f32),
            pltpu.VMEM((size // n // 2, n2, size), f32),
            pltpu.VMEM((size // n // 2, n2, size), f32),
            pltpu.VMEM((n2, size), f32),
            pltpu.VMEM((n2 // 2, size), f32),
            pltpu.VMEM((n // 2 - 1, n2 // n, size), f32),
            pltpu.VMEM((n2, size), f32),
            pltpu.SemaphoreType.DMA((9,)),
            pltpu.SemaphoreType.DMA((9,)),
        ],
        compiler_params=pltpu.CompilerParams(
            collective_id=0, has_side_effects=True, vmem_limit_bytes=32 * 1024 * 1024
        ),
        cost_estimate=pl.CostEstimate(
            flops=600_000_000, bytes_accessed=2_000_000, transcendentals=256
        ),
    )(field, sketch_one, sketch_two, ranks)


def solution(mesh):
    n = mesh.shape["wide"]

    def per_device(field, sketch_one, sketch_two, ranks):
        ydev, kdim, n1 = field.shape
        n2, size = sketch_two.shape
        fits = (
            mesh.shape["narrow"] == 1
            and size == 128
            and n % 2 == 0
            and n >= 4
            and ydev == 8
            and kdim <= size // 2
            and size % (2 * n) == 0
            and n1 % (8 * n) == 0
            and n2 == 8 * n
        )
        if fits:
            return fused(n, field, sketch_one, sketch_two, ranks)
        return general(field, sketch_one, sketch_two, ranks)

    return jax.shard_map(
        per_device,
        mesh=mesh,
        in_specs=(P("wide", "narrow", None), P(), P(), P()),
        out_specs=P("wide", "narrow", None),
        check_vma=False,
    )
```

profile of v0, /device:TPU:0, one launch (start us, length us, event | category | flops | bytes accessed | tf_op | source)
XLA Modules:
  0.0 53.2 jit_solution(11028414127946319123)
XLA Ops:
  0.0 0.0 copy-start.2
  0.0 0.0 copy-start.1
  0.0 0.0 copy-start
  0.0 1.6 %copy.5.field = f32[8,44,512]{2,1,0:T(8,128)S(1)} copy(f32[8,44,512]{2,0,1:T(8,128)} %param.4) | data formatting | bytes 1441792 | tf_op args[0]
  1.6 0.0 copy-done.2
  1.6 0.0 copy-done.1
  1.6 0.0 copy-done
  1.6 50.9 %shard_map.46 = f32[4,44,128]{2,1,0:T(8,128)S(1)} custom-call(f32[8,44,512]{2,1,0:T(8,128)S(1)} %copy.5.field, f32[512,128]{1,0:T(8,128)S(1)} %copy-done, f32[256,128]{1,0:T(8,128)S(1)} %copy-done.1, s32[2]{0:T(128)S(1)} %copy-done.2), custom_call_target="tpu_custom_call" | custom-call | flops 600000000 | bytes 2000000 | tf_op jit(solution)/shard_map/pallas_call | solution.py:272
  52.6 0.7 %copy.6 = f32[4,44,128]{2,0,1:T(4,128)} copy(f32[4,44,128]{2,1,0:T(8,128)S(1)} %shard_map.46) | data formatting | bytes 180224 | tf_op jit(solution)/shard_map/pallas_call | solution.py:272
Async XLA Ops:
  0.0 1.6 %copy-start.2 = (s32[2]{0:T(128)S(1)}, s32[2]{0:T(128)}, u32[]{:S(2)}) copy-start(s32[2]{0:T(128)} %ranks.1) | copy-start | bytes 28
  0.0 1.6 %copy-start.1 = (f32[256,128]{1,0:T(8,128)S(1)}, f32[256,128]{1,0:T(8,128)}, u32[]{:S(2)}) copy-start(f32[256,128]{1,0:T(8,128)} %sketch_two.1) | copy-start | bytes 393220
  0.0 1.6 %copy-start = (f32[512,128]{1,0:T(8,128)S(1)}, f32[512,128]{1,0:T(8,128)}, u32[]{:S(2)}) copy-start(f32[512,128]{1,0:T(8,128)} %sketch_one.1) | copy-start | bytes 786436
where the time goes:
time: 53.4 us; the launch traced here: 53.2 us
  Pallas kernels  50.9 us (95%)
  local copies, waits for them, and re-layouts  2.27 us (4%)
    pallas_call x1, Pallas kernels, fused(): pl.pallas_call(functools.partial(kernel, n), out_shape=jax.ShapeDtypeStru...  50.9 us
    unnamed x7, local copies, waits for them, and re-layouts  1.59 us

commit v1 on v0

v1 whole, which is shorter than its diff:
```python
import functools

import jax
import jax.numpy as jnp
from jax import lax
from jax.experimental import pallas as pl
from jax.experimental.pallas import tpu as pltpu
from jax.sharding import PartitionSpec as P

HIGHEST = lax.Precision.HIGHEST
MESH = pl.DeviceIdType.MESH


def make_basis(local, sketch, rank):
    keep = (jnp.arange(sketch.shape[1]) < rank).astype(jnp.float32)
    masked = sketch * keep
    part = jnp.einsum("akn,ns->aks", local, masked, precision=HIGHEST)
    part = jnp.einsum("akn,aks->ns", local, part, precision=HIGHEST)
    sketched = lax.psum(part, ("wide", "narrow"))
    inner = jnp.dot(sketched.T, sketched, precision=HIGHEST) + jnp.diag(1.0 - keep)
    lower = jnp.linalg.cholesky(inner)
    return jax.scipy.linalg.solve_triangular(lower, sketched.T, lower=True)


def general(field, sketch_one, sketch_two, ranks):
    basis_one = make_basis(field, sketch_one, ranks[0])
    core_one = jnp.einsum("rn,ykn->rky", basis_one, field, precision=HIGHEST)
    regrouped = lax.all_to_all(core_one, "wide", split_axis=0, concat_axis=2, tiled=True)
    basis_two = make_basis(regrouped, sketch_two, ranks[1])
    return jnp.einsum("sn,rkn->rks", basis_two, regrouped, precision=HIGHEST)


def dot(a, b, dims):
    return lax.dot_general(
        a, b, (dims, ((), ())), precision=HIGHEST, preferred_element_type=jnp.float32
    )


NN = ((1,), (0,))
NT = ((1,), (1,))
TN = ((0,), (0,))
BLOCK = 8
TILES = 4
KB = 2
PLANE = 8
USED = 6


def inverse_factor(work, linv):
    size = linv.shape[0]
    tile = (BLOCK, size)
    group = TILES * BLOCK
    sub = lax.broadcasted_iota(jnp.int32, tile, 0)

    for r0 in range(0, size, group):
        own = work[r0 : r0 + group, :size]
        rest = work[r0 : r0 + group, size:]
        rows_a = [own[u * BLOCK : (u + 1) * BLOCK, :] for u in range(TILES)]
        rows_t = [rest[u * BLOCK : (u + 1) * BLOCK, :] for u in range(TILES)]
        panels_a, panels_t = [], []
        for u in range(TILES):
            d, below = {}, {}
            for q in range(BLOCK):
                lane = r0 + u * BLOCK + q
                column = jnp.broadcast_to(rows_a[u][:, lane : lane + 1], tile)
                for p in range(q, BLOCK):
                    d[p, q] = jnp.broadcast_to(column[p : p + 1, :], tile)
                for v in range(u + 1, TILES):
                    below[v, q] = jnp.broadcast_to(rows_a[v][:, lane : lane + 1], tile)
            done_a, done_t = [], []
            panel_a = jnp.zeros(tile, jnp.float32)
            panel_t = jnp.zeros(tile, jnp.float32)
            for j in range(BLOCK):
                x = d[j, j]
                y = lax.rsqrt(x)
                y = y * (1.5 - 0.5 * ((x * y) * y))
                for p in range(j + 1, BLOCK):
                    d[p, j] = d[p, j] * y
                for v in range(u + 1, TILES):
                    below[v, j] = below[v, j] * y
                for q in range(j + 1, BLOCK):
                    for p in range(q, BLOCK):
                        d[p, q] = d[p, q] - d[p, j] * d[q, j]
                    for v in range(u + 1, TILES):
                        below[v, q] = below[v, q] - below[v, j] * d[q, j]
                ra = jnp.broadcast_to(rows_a[u][j : j + 1, :], tile)
                rt = jnp.broadcast_to(rows_t[u][j : j + 1, :], tile)
                for k in range(j):
                    ra = ra - d[j, k] * done_a[k]
                    rt = rt - d[j, k] * done_t[k]
                ra = ra * y
                rt = rt * y
                done_a.append(ra)
                done_t.append(rt)
                panel_a = jnp.where(sub == j, ra, panel_a)
                panel_t = jnp.where(sub == j, rt, panel_t)
                for v in range(u + 1, TILES):
                    rows_a[v] = rows_a[v] - below[v, j] * ra
                    rows_t[v] = rows_t[v] - below[v, j] * rt
            panels_a.append(panel_a)
            panels_t.append(panel_t)
        panel_t = jnp.concatenate(panels_t, axis=0)
        panel_a = jnp.concatenate(panels_a, axis=0)
        linv[r0 : r0 + group, :] = panel_t
        end = r0 + group
        if end < size:
            both = jnp.concatenate([panel_a, panel_t], axis=1)
            work[end:, :] = work[end:, :] - dot(panel_a.T[end:, :], both, NN)


def fill_work(work, inner, keep_row, size):
    row = lax.broadcasted_iota(jnp.int32, (size, size), 0)
    col = lax.broadcasted_iota(jnp.int32, (size, size), 1)
    eye = (row == col).astype(jnp.float32)
    work[:, :size] = inner + eye * (1.0 - keep_row)
    work[:, size:] = eye


def far_first(bits, low):
    def hops(m):
        flat = sum((m >> b) & 1 for b in range(low))
        return flat + (m >> low)

    return sorted(range(1, 1 << bits), key=lambda m: -hops(m))


def kernel(
    n, field, sketch_one, sketch_two, ranks_in, out,
    flat, s1, s2, ranks, part, pair, mine, got, full, rot, have, work, linv, stack,
    part_two, pair_two, mine_two, got_two, full_two, give, last,
    load_sem, send_sem, recv_sem,
):
    me = lax.axis_index("wide")
    size = s1.shape[1]
    wide = flat.shape[2]
    holders = rot.shape[0] // KB
    ydev = rot.shape[1]
    n2 = s2.shape[0]
    per = size // n
    chips = n // 2
    rows = size // chips
    core = lax.rem(me, 2)
    chip = me // 2

    loads = [
        pltpu.make_async_copy(ranks_in, ranks, load_sem.at[0]),
        pltpu.make_async_copy(sketch_one, s1, load_sem.at[1]),
        pltpu.make_async_copy(field.at[:, pl.ds(0, wide)], flat.at[0], load_sem.at[2]),
        pltpu.make_async_copy(field.at[:, pl.ds(wide, wide)], flat.at[1], load_sem.at[3]),
        pltpu.make_async_copy(sketch_two, s2, load_sem.at[4]),
    ]
    for load in loads:
        load.start()

    barrier = pltpu.get_barrier_semaphore()

    def greet(i, carry):
        peer = lax.rem(me + 1 + i, n)
        pl.semaphore_signal(barrier, inc=1, device_id={"wide": peer}, device_id_type=MESH)
        return carry

    lax.fori_loop(0, n - 1, greet, 0)

    bits = n.bit_length() - 1
    deltas = [(1 - 2 * lax.rem(me // (1 << b), 2)) * (1 << b) for b in range(bits)]

    def flipped(m):
        return me + sum(deltas[b] for b in range(bits) if (m >> b) & 1)

    alike = [(2 * m, flipped(2 * m)) for m in far_first(bits - 1, 2)]
    every = [(m, flipped(m)) for m in far_first(bits, 3)]
    twin = flipped(1)

    def copy(phase, source, target, peer):
        return pltpu.make_async_remote_copy(
            src_ref=source, dst_ref=target,
            send_sem=send_sem.at[phase], recv_sem=recv_sem.at[phase],
            device_id={"wide": peer}, device_id_type=MESH,
        )

    def of_chip(c):
        return pl.ds(pl.multiple_of(c * rows, rows), rows)

    slot = (me // PLANE) * USED + lax.rem(me, PLANE)
    holds = jnp.logical_and(lax.rem(me, PLANE) < USED, slot < holders)
    idle = jnp.logical_not(holds)

    loads[0].wait()
    lane = lax.broadcasted_iota(jnp.int32, (1, size), 1)
    sub = lax.broadcasted_iota(jnp.int32, (size, 1), 0)
    keep_one = (lane < ranks[0]).astype(jnp.float32)
    keep_two = (lane < ranks[1]).astype(jnp.float32)
    loads[1].wait()
    turned = s1[...].T * (sub < ranks[0]).astype(jnp.float32)
    loads[2].wait()
    projected = dot(turned[:, :wide], flat[0], NT)
    loads[3].wait()
    projected = projected + dot(turned[:, wide:], flat[1], NT)
    part[1 - core] = dot(projected, flat[1 - core], NN)

    pl.semaphore_wait(barrier, n - 1)

    copy(0, part.at[1 - core], pair, twin).start()
    part[core] = dot(projected, flat[core], NN)
    copy(0, pair, pair, twin).wait_recv()
    mine[...] = part[core] + pair[...]
    for i, (m, peer) in enumerate(alike):
        copy(1, mine.at[of_chip(peer // 2), :], got.at[m // 2 - 1], peer).start()
    loads[4].wait()
    masked_two = (s2[...].T) * (sub < ranks[1]).astype(jnp.float32)
    s2t = masked_two
    copy(1, got, got, twin).wait_recv()
    full[core, of_chip(chip), :] = jnp.sum(got[...], axis=0) + mine[of_chip(chip), :]
    for m, peer in alike:
        own = full.at[core, of_chip(chip), :]
        copy(2, own, own, peer).start()
    copy(2, got, got, twin).wait_recv()
    copy(3, full.at[core], full.at[core], twin).start()
    sk = full[core]
    turn = dot(flat[core], sk, NT)
    inner = dot(sk, sk, NT)
    copy(3, pair, pair, twin).wait_recv()
    sk = full[1 - core]
    turn = turn + dot(flat[1 - core], sk, NT)
    rot[...] = turn.reshape(rot.shape)

    mine_y = pl.ds(pl.multiple_of(me * ydev, ydev), ydev)
    planes = n // PLANE
    plane = me // PLANE
    for t in range(planes):
        far = planes - 1 - t
        there = plane + sum(
            (deltas[3 + b] // PLANE) for b in range(bits - 3) if (far >> b) & 1
        )
        for i in range(USED):
            inside = lax.rem(lax.rem(me, PLANE) + 1 + i, USED)
            j = there * USED + inside
            peer = there * PLANE + inside

            @pl.when(jnp.logical_and(j < holders, peer != me))
            def _():
                copy(
                    4, rot.at[pl.ds(KB * j, KB)], have.at[:, mine_y, :], peer
                ).start()

    @pl.when(holds)
    def _():
        have[:, mine_y, :] = rot[pl.ds(KB * slot, KB)]

    inner = inner + dot(sk, sk, NT)
    fill_work(work, inner, keep_one, size)
    inverse_factor(work, linv)

    half_two = n2 // 2
    holder_chips = holders // 2

    @pl.when(holds)
    def _():
        everything = have.at[:, pl.ds(0, n2 - ydev), :]
        copy(4, everything, everything, twin).wait_recv()
        for k in range(KB):
            stack[k * size : (k + 1) * size, :] = dot(linv[...], have[k], NT)
        mixed = stack[...]
        spread = dot(s2t, mixed, NT)
        total = dot(spread, mixed, NN)
        part_two[0] = total[:, :half_two]
        part_two[1] = total[:, half_two:]
        copy(5, part_two.at[1 - core], pair_two, twin).start()
        copy(5, pair_two, pair_two, twin).wait_recv()
        mine_two[...] = part_two[core] + pair_two[...]
        for m, peer in alike:
            copy(
                6, mine_two.at[of_chip(peer // 2), :], got_two.at[slot // 2], peer
            ).start()
        got_two[slot // 2] = mine_two[of_chip(chip), :]
        all_but_one = got_two.at[pl.ds(0, holder_chips - 1)]
        copy(6, all_but_one, all_but_one, twin).wait_recv()

    @pl.when(idle)
    def _():
        copy(6, got_two, got_two, twin).wait_recv()

    lanes = pl.ds(pl.multiple_of(core * half_two, half_two), half_two)
    own = full_two.at[of_chip(chip), lanes]
    own[...] = jnp.sum(got_two[...], axis=0)
    for m, peer in every:
        copy(7, own, own, peer).start()
    others = give.at[pl.ds(0, n - 1)]
    copy(7, others, others, twin).wait_recv()

    sk = full_two[...]
    low = lax.broadcasted_iota(jnp.int32, (KB * per, size), 0) < per

    @pl.when(holds)
    def _():
        spun = dot(stack[...], full_two[...], NT)
        for t in range(n // 2):
            first = spun[KB * per * t : KB * per * (t + 1), :]
            second = spun[size + KB * per * t : size + KB * per * (t + 1), :]
            give[2 * t] = jnp.where(low, first, pltpu.roll(second, per, 0))
            give[2 * t + 1] = jnp.where(low, pltpu.roll(first, per, 0), second)
        for m, peer in every:
            copy(8, give.at[peer], last.at[slot], peer).start()
        last[slot] = give[me]

    fill_work(work, dot(sk, sk, NT), keep_two, size)
    inverse_factor(work, linv)

    @pl.when(holds)
    def _():
        most = last.at[pl.ds(0, holders - 1)]
        copy(8, most, most, twin).wait_recv()

    @pl.when(idle)
    def _():
        copy(8, last, last, twin).wait_recv()

    out[...] = dot(last[...].reshape(out.shape), linv[...], NT)

    copy(0, pair, pair, twin).wait_send()
    copy(1, got, got, twin).wait_send()
    copy(2, got, got, twin).wait_send()
    copy(3, pair, pair, twin).wait_send()
    copy(7, others, others, twin).wait_send()

    @pl.when(holds)
    def _():
        most = rot.at[pl.ds(0, KB * (holders - 1))]
        copy(4, most, most, twin).wait_send()
        copy(5, pair_two, pair_two, twin).wait_send()
        most = mine_two.at[pl.ds(0, size - rows), :]
        copy(6, most, most, twin).wait_send()
        most = give.at[pl.ds(0, n - 1)]
        copy(8, most, most, twin).wait_send()

    @pl.when(idle)
    def _():
        copy(4, rot, rot, twin).wait_send()


def fused(n, field, sketch_one, sketch_two, ranks):
    ydev, kdim, n1 = field.shape
    n2, size = sketch_two.shape
    chips = n // 2
    rows = size // chips
    wide = n1 // 2
    holders = kdim // KB
    per = size // n
    hbm = pl.BlockSpec(memory_space=pltpu.MemorySpace.HBM)
    f32 = jnp.float32
    lines = jnp.transpose(field, (1, 0, 2)).reshape(kdim * ydev, n1)
    core = pl.pallas_call(
        functools.partial(kernel, n),
        out_shape=jax.ShapeDtypeStruct((kdim * per, size), f32),
        in_specs=[hbm, hbm, hbm, hbm],
        out_specs=pl.BlockSpec(memory_space=pltpu.VMEM),
        scratch_shapes=[
            pltpu.VMEM((2, kdim * ydev, wide), f32),
            pltpu.VMEM((n1, size), f32),
            pltpu.VMEM((n2, size), f32),
            pltpu.SMEM((2,), jnp.int32),
            pltpu.VMEM((2, size, wide), f32),
            pltpu.VMEM((size, wide), f32),
            pltpu.VMEM((size, wide), f32),
            pltpu.VMEM((chips - 1, rows, wide), f32),
            pltpu.VMEM((2, size, wide), f32),
            pltpu.VMEM((kdim, ydev, size), f32),
            pltpu.VMEM((KB, n2, size), f32),
            pltpu.VMEM((size, 2 * size), f32),
            pltpu.VMEM((size, size), f32),
            pltpu.VMEM((KB * size, n2), f32),
            pltpu.VMEM((2, size, n2 // 2), f32),
            pltpu.VMEM((size, n2 // 2), f32),
            pltpu.VMEM((size, n2 // 2), f32),
            pltpu.VMEM((holders // 2, rows, n2 // 2), f32),
            pltpu.VMEM((size, n2), f32),
            pltpu.VMEM((n, KB * per, size), f32),
            pltpu.VMEM((holders, KB * per, size), f32),
            pltpu.SemaphoreType.DMA((5,)),
            pltpu.SemaphoreType.DMA((9,)),
            pltpu.SemaphoreType.DMA((9,)),
        ],
        compiler_params=pltpu.CompilerParams(
            collective_id=0, has_side_effects=True, vmem_limit_bytes=56 * 1024 * 1024
        ),
        cost_estimate=pl.CostEstimate(
            flops=600_000_000, bytes_accessed=2_000_000, transcendentals=256
        ),
    )(lines, sketch_one, sketch_two, ranks)
    return jnp.transpose(core.reshape(kdim, per, size), (1, 0, 2))


def solution(mesh):
    n = mesh.shape["wide"]

    def per_device(field, sketch_one, sketch_two, ranks):
        ydev, kdim, n1 = field.shape
        n2, size = sketch_two.shape
        fits = (
            mesh.shape["narrow"] == 1
            and size == 128
            and n == 32
            and ydev == 8
            and kdim % (2 * KB) == 0
            and kdim // KB <= n // PLANE * USED
            and n1 == 512
            and n2 == 8 * n
        )
        if fits:
            return fused(n, field, sketch_one, sketch_two, ranks)
        return general(field, sketch_one, sketch_two, ranks)

    return jax.shard_map(
        per_device,
        mesh=mesh,
        in_specs=(P("wide", "narrow", None), P(), P(), P()),
        out_specs=P("wide", "narrow", None),
        check_vma=False,
    )
```

time: 53.4 us -> 45.9 us (0.86)
  Pallas kernels: 50.9 us -> 44.2 us
  local copies, waits for them, and re-layouts: 2.27 us -> 1.53 us
    pallas_call x1, Pallas kernels: 50.9 us -> 44.2 us  [fused(): pl.pallas_call(functools.partial(kernel, n), out_shape=jax.ShapeDtypeStru...]
    pallas_call x1 -> x0, local copies, waits for them, and re-layouts: 0.67 us -> none  [fused(): pl.pallas_call(functools.partial(kernel, n), out_shape=jax.ShapeDtypeStru...]
    unnamed x7 -> x1, local copies, waits for them, and re-layouts: 1.59 us -> 1.53 us
where the time goes in v1:
time: 45.9 us; the launch traced here: 45.7 us
  Pallas kernels  44.2 us (96%)
  local copies, waits for them, and re-layouts  1.53 us (3%)
    pallas_call x1, Pallas kernels, fused(): pl.pallas_call(functools.partial(kernel, n), out_shape=jax.ShapeDtypeStru...  44.2 us
    unnamed x1, local copies, waits for them, and re-layouts  1.53 us

profile of v1, /device:TPU:0, one launch (start us, length us, event | category | flops | bytes accessed | tf_op | source)
XLA Modules:
  0.0 45.7 jit_solution(16772641084304503008)
XLA Ops:
  0.0 44.2 %shard_map.46 = f32[176,128]{1,0:T(8,128)} custom-call(f32[352,512]{1,0:T(8,128)} %bitcast.7, f32[512,128]{1,0:T(8,128)} %sketch_one.1, f32[256,128]{1,0:T(8,128)} %sketch_two.1, s32[2]{0:T(128)} %ranks_in.1), custom_call_target="tpu_custom_call" | custom-call | flops 600000000 | bytes 2000000 | tf_op jit(solution)/shard_map/pallas_call | solution.py:352
  44.2 1.5 %copy.6 = f32[4,44,128]{2,0,1:T(4,128)} copy(f32[4,44,128]{2,0,1:T(4,128)} %bitcast.6) | data formatting | bytes 180224

commit v2 on v1

--- a/solution.py
+++ b/solution.py
@@ -41,9 +41,8 @@
 TN = ((0,), (0,))
 BLOCK = 8
 TILES = 4
-KB = 2
+KB = 3
 PLANE = 8
-USED = 6
 
 
 def inverse_factor(work, linv):
@@ -127,13 +126,14 @@
 def kernel(
     n, field, sketch_one, sketch_two, ranks_in, out,
     flat, s1, s2, ranks, part, pair, mine, got, full, rot, have, work, linv, stack,
-    part_two, pair_two, mine_two, got_two, full_two, give, last,
+    part_two, got_two, full_two, give, last,
     load_sem, send_sem, recv_sem,
 ):
     me = lax.axis_index("wide")
     size = s1.shape[1]
     wide = flat.shape[2]
-    holders = rot.shape[0] // KB
+    holders = last.shape[0]
+    lines = field.shape[0]
     ydev = rot.shape[1]
     n2 = s2.shape[0]
     per = size // n
@@ -145,8 +145,14 @@
     loads = [
         pltpu.make_async_copy(ranks_in, ranks, load_sem.at[0]),
         pltpu.make_async_copy(sketch_one, s1, load_sem.at[1]),
-        pltpu.make_async_copy(field.at[:, pl.ds(0, wide)], flat.at[0], load_sem.at[2]),
-        pltpu.make_async_copy(field.at[:, pl.ds(wide, wide)], flat.at[1], load_sem.at[3]),
+    ] + [
+        pltpu.make_async_copy(
+            field.at[:, pl.ds(wide * h, wide)],
+            flat.at[h, pl.ds(0, lines), :],
+            load_sem.at[2 + h],
+        )
+        for h in range(2)
+    ] + [
         pltpu.make_async_copy(sketch_two, s2, load_sem.at[4]),
     ]
     for load in loads:
@@ -168,7 +174,6 @@
         return me + sum(deltas[b] for b in range(bits) if (m >> b) & 1)
 
     alike = [(2 * m, flipped(2 * m)) for m in far_first(bits - 1, 2)]
-    every = [(m, flipped(m)) for m in far_first(bits, 3)]
     twin = flipped(1)
 
     def copy(phase, source, target, peer):
@@ -178,13 +183,35 @@
             device_id={"wide": peer}, device_id_type=MESH,
         )
 
+    waits = []
+
+    def later(phase, sent, when=None):
+        def wait():
+            copy(phase, sent, sent, twin).wait_send()
+
+        waits.append(wait if when is None else functools.partial(pl.when(when), wait))
+
     def of_chip(c):
         return pl.ds(pl.multiple_of(c * rows, rows), rows)
 
-    slot = (me // PLANE) * USED + lax.rem(me, PLANE)
-    holds = jnp.logical_and(lax.rem(me, PLANE) < USED, slot < holders)
-    idle = jnp.logical_not(holds)
-
+    plane = me // PLANE
+    below = me - plane * PLANE
+    middle = jnp.logical_or(plane == 1, plane == 2)
+    outside = jnp.logical_not(middle)
+    slot = jnp.clip(me - PLANE, 0, 2 * PLANE - 1)
+    holds = jnp.logical_and(middle, slot < holders)
+    spare = jnp.logical_not(holds)
+    turns = (6, 7, 4, 5, 2, 3, 1, 0)
+    inside = [below + sum(deltas[b] for b in range(3) if (m >> b) & 1) for m in turns]
+    nearer = jnp.where(plane < 2, PLANE, 2 * PLANE)
+    farther = 3 * PLANE - nearer
+    group = [b + farther for b in inside] + [b + nearer for b in inside[:-1]]
+    edges = [b + 3 * (farther - PLANE) for b in inside] + [
+        b + 3 * (nearer - PLANE) for b in inside
+    ]
+
+    for h in range(2):
+        flat[h, lines:, :] = jnp.zeros((flat.shape[1] - lines, wide), jnp.float32)
     loads[0].wait()
     lane = lax.broadcasted_iota(jnp.int32, (1, size), 1)
     sub = lax.broadcasted_iota(jnp.int32, (size, 1), 0)
@@ -193,19 +220,20 @@
     loads[1].wait()
     turned = s1[...].T * (sub < ranks[0]).astype(jnp.float32)
     loads[2].wait()
-    projected = dot(turned[:, :wide], flat[0], NT)
+    projected = dot(turned[:, :wide], flat[0, :lines, :], NT)
     loads[3].wait()
-    projected = projected + dot(turned[:, wide:], flat[1], NT)
-    part[1 - core] = dot(projected, flat[1 - core], NN)
+    projected = projected + dot(turned[:, wide:], flat[1, :lines, :], NT)
+    part[1 - core] = dot(projected, flat[1 - core, pl.ds(0, lines), :], NN)
 
     pl.semaphore_wait(barrier, n - 1)
-
     copy(0, part.at[1 - core], pair, twin).start()
-    part[core] = dot(projected, flat[core], NN)
+    later(0, pair)
+    part[core] = dot(projected, flat[core, pl.ds(0, lines), :], NN)
     copy(0, pair, pair, twin).wait_recv()
     mine[...] = part[core] + pair[...]
     for i, (m, peer) in enumerate(alike):
         copy(1, mine.at[of_chip(peer // 2), :], got.at[m // 2 - 1], peer).start()
+    later(1, got)
     loads[4].wait()
     masked_two = (s2[...].T) * (sub < ranks[1]).astype(jnp.float32)
     s2t = masked_two
@@ -214,28 +242,27 @@
     for m, peer in alike:
         own = full.at[core, of_chip(chip), :]
         copy(2, own, own, peer).start()
+    later(2, got)
     copy(2, got, got, twin).wait_recv()
     copy(3, full.at[core], full.at[core], twin).start()
+    later(3, pair)
     sk = full[core]
-    turn = dot(flat[core], sk, NT)
+    rot[...] = dot(flat[core], sk, NT).reshape(rot.shape)
     inner = dot(sk, sk, NT)
     copy(3, pair, pair, twin).wait_recv()
     sk = full[1 - core]
-    turn = turn + dot(flat[1 - core], sk, NT)
-    rot[...] = turn.reshape(rot.shape)
 
     mine_y = pl.ds(pl.multiple_of(me * ydev, ydev), ydev)
-    planes = n // PLANE
-    plane = me // PLANE
-    for t in range(planes):
-        far = planes - 1 - t
-        there = plane + sum(
-            (deltas[3 + b] // PLANE) for b in range(bits - 3) if (far >> b) & 1
-        )
-        for i in range(USED):
-            inside = lax.rem(lax.rem(me, PLANE) + 1 + i, USED)
-            j = there * USED + inside
-            peer = there * PLANE + inside
+    part_lines = PLANE * KB * ydev
+    for base in (farther, nearer):
+        first = base - PLANE
+        ks = pl.ds(KB * first, KB * PLANE)
+        span = pl.ds(pl.multiple_of(first * (KB * ydev), part_lines), part_lines)
+        more = dot(flat[1 - core, span, :], sk, NT)
+        rot[ks] = rot[ks] + more.reshape(KB * PLANE, ydev, size)
+        for b in inside:
+            peer = b + base
+            j = peer - PLANE
 
             @pl.when(jnp.logical_and(j < holders, peer != me))
             def _():
@@ -243,6 +270,9 @@
                     4, rot.at[pl.ds(KB * j, KB)], have.at[:, mine_y, :], peer
                 ).start()
 
+    later(4, rot.at[pl.ds(0, KB * (holders - 1))], holds)
+    later(4, rot.at[pl.ds(0, KB * holders)], spare)
+
     @pl.when(holds)
     def _():
         have[:, mine_y, :] = rot[pl.ds(KB * slot, KB)]
@@ -251,58 +281,67 @@
     fill_work(work, inner, keep_one, size)
     inverse_factor(work, linv)
 
-    half_two = n2 // 2
-    holder_chips = holders // 2
-
     @pl.when(holds)
     def _():
         everything = have.at[:, pl.ds(0, n2 - ydev), :]
         copy(4, everything, everything, twin).wait_recv()
+
+    @pl.when(holds)
+    def _():
         for k in range(KB):
             stack[k * size : (k + 1) * size, :] = dot(linv[...], have[k], NT)
         mixed = stack[...]
         spread = dot(s2t, mixed, NT)
         total = dot(spread, mixed, NN)
-        part_two[0] = total[:, :half_two]
-        part_two[1] = total[:, half_two:]
-        copy(5, part_two.at[1 - core], pair_two, twin).start()
-        copy(5, pair_two, pair_two, twin).wait_recv()
-        mine_two[...] = part_two[core] + pair_two[...]
-        for m, peer in alike:
-            copy(
-                6, mine_two.at[of_chip(peer // 2), :], got_two.at[slot // 2], peer
-            ).start()
-        got_two[slot // 2] = mine_two[of_chip(chip), :]
-        all_but_one = got_two.at[pl.ds(0, holder_chips - 1)]
-        copy(6, all_but_one, all_but_one, twin).wait_recv()
-
-    @pl.when(idle)
+        part_two[...] = total
+
+    def of_slot(j):
+        return pl.ds(pl.multiple_of(j * rows, rows), rows)
+
+    @pl.when(holds)
+    def _():
+        for peer in group:
+            copy(6, part_two.at[of_slot(peer - PLANE), :], got_two.at[slot], peer).start()
+        got_two[slot] = part_two[of_slot(slot), :]
+        most = got_two.at[pl.ds(0, holders - 1)]
+        copy(6, most, most, twin).wait_recv()
+
+    @pl.when(jnp.logical_and(middle, spare))
     def _():
         copy(6, got_two, got_two, twin).wait_recv()
 
-    lanes = pl.ds(pl.multiple_of(core * half_two, half_two), half_two)
-    own = full_two.at[of_chip(chip), lanes]
-    own[...] = jnp.sum(got_two[...], axis=0)
-    for m, peer in every:
-        copy(7, own, own, peer).start()
-    others = give.at[pl.ds(0, n - 1)]
-    copy(7, others, others, twin).wait_recv()
-
-    sk = full_two[...]
-    low = lax.broadcasted_iota(jnp.int32, (KB * per, size), 0) < per
+    later(6, part_two.at[pl.ds(0, size - rows), :], holds)
+    most_two = full_two.at[pl.ds(0, size - rows), :]
+
+    @pl.when(middle)
+    def _():
+        own = full_two.at[of_slot(slot), :]
+        own[...] = jnp.sum(got_two[...], axis=0)
+        for peer in group:
+            copy(7, own, own, peer).start()
+        for peer in edges:
+            copy(5, own, own, peer).start()
+        copy(7, most_two, most_two, twin).wait_recv()
+
+    @pl.when(outside)
+    def _():
+        copy(5, full_two, full_two, twin).wait_recv()
+
+    later(7, most_two, middle)
+    later(5, full_two, middle)
 
     @pl.when(holds)
     def _():
         spun = dot(stack[...], full_two[...], NT)
-        for t in range(n // 2):
-            first = spun[KB * per * t : KB * per * (t + 1), :]
-            second = spun[size + KB * per * t : size + KB * per * (t + 1), :]
-            give[2 * t] = jnp.where(low, first, pltpu.roll(second, per, 0))
-            give[2 * t + 1] = jnp.where(low, pltpu.roll(first, per, 0), second)
-        for m, peer in every:
+        for d in range(n):
+            for k in range(KB):
+                give[d, k] = spun[k * size + per * d : k * size + per * (d + 1), :]
+        for peer in edges + group:
             copy(8, give.at[peer], last.at[slot], peer).start()
         last[slot] = give[me]
 
+    later(8, give.at[pl.ds(0, n - 1)], holds)
+    sk = full_two[...]
     fill_work(work, dot(sk, sk, NT), keep_two, size)
     inverse_factor(work, linv)
 
@@ -311,31 +350,15 @@
         most = last.at[pl.ds(0, holders - 1)]
         copy(8, most, most, twin).wait_recv()
 
-    @pl.when(idle)
+    @pl.when(spare)
     def _():
         copy(8, last, last, twin).wait_recv()
 
-    out[...] = dot(last[...].reshape(out.shape), linv[...], NT)
-
-    copy(0, pair, pair, twin).wait_send()
-    copy(1, got, got, twin).wait_send()
-    copy(2, got, got, twin).wait_send()
-    copy(3, pair, pair, twin).wait_send()
-    copy(7, others, others, twin).wait_send()
-
-    @pl.when(holds)
-    def _():
-        most = rot.at[pl.ds(0, KB * (holders - 1))]
-        copy(4, most, most, twin).wait_send()
-        copy(5, pair_two, pair_two, twin).wait_send()
-        most = mine_two.at[pl.ds(0, size - rows), :]
-        copy(6, most, most, twin).wait_send()
-        most = give.at[pl.ds(0, n - 1)]
-        copy(8, most, most, twin).wait_send()
-
-    @pl.when(idle)
-    def _():
-        copy(4, rot, rot, twin).wait_send()
+    done = dot(last[...].reshape(holders * KB * per, size), linv[...], NT)
+    out[...] = done[: out.shape[0], :]
+
+    for wait in waits:
+        wait()
 
 
 def fused(n, field, sketch_one, sketch_two, ranks):
@@ -344,7 +367,8 @@
     chips = n // 2
     rows = size // chips
     wide = n1 // 2
-    holders = kdim // KB
+    holders = -(-kdim // KB)
+    padded = 2 * PLANE * KB
     per = size // n
     hbm = pl.BlockSpec(memory_space=pltpu.MemorySpace.HBM)
     f32 = jnp.float32
@@ -355,7 +379,7 @@
         in_specs=[hbm, hbm, hbm, hbm],
         out_specs=pl.BlockSpec(memory_space=pltpu.VMEM),
         scratch_shapes=[
-            pltpu.VMEM((2, kdim * ydev, wide), f32),
+            pltpu.VMEM((2, padded * ydev, wide), f32),
             pltpu.VMEM((n1, size), f32),
             pltpu.VMEM((n2, size), f32),
             pltpu.SMEM((2,), jnp.int32),
@@ -364,24 +388,22 @@
             pltpu.VMEM((size, wide), f32),
             pltpu.VMEM((chips - 1, rows, wide), f32),
             pltpu.VMEM((2, size, wide), f32),
-            pltpu.VMEM((kdim, ydev, size), f32),
+            pltpu.VMEM((padded, ydev, size), f32),
             pltpu.VMEM((KB, n2, size), f32),
             pltpu.VMEM((size, 2 * size), f32),
             pltpu.VMEM((size, size), f32),
             pltpu.VMEM((KB * size, n2), f32),
-            pltpu.VMEM((2, size, n2 // 2), f32),
-            pltpu.VMEM((size, n2 // 2), f32),
-            pltpu.VMEM((size, n2 // 2), f32),
-            pltpu.VMEM((holders // 2, rows, n2 // 2), f32),
             pltpu.VMEM((size, n2), f32),
-            pltpu.VMEM((n, KB * per, size), f32),
-            pltpu.VMEM((holders, KB * per, size), f32),
+            pltpu.VMEM((holders, rows, n2), f32),
+            pltpu.VMEM((size, n2), f32),
+            pltpu.VMEM((n, KB, per, size), f32),
+            pltpu.VMEM((holders, KB, per, size), f32),
             pltpu.SemaphoreType.DMA((5,)),
             pltpu.SemaphoreType.DMA((9,)),
             pltpu.SemaphoreType.DMA((9,)),
         ],
         compiler_params=pltpu.CompilerParams(
-            collective_id=0, has_side_effects=True, vmem_limit_bytes=56 * 1024 * 1024
+            collective_id=0, has_side_effects=True, vmem_limit_bytes=55075 * 1024
         ),
         cost_estimate=pl.CostEstimate(
             flops=600_000_000, bytes_accessed=2_000_000, transcendentals=256
@@ -401,8 +423,8 @@
             and size == 128
             and n == 32
             and ydev == 8
-            and kdim % (2 * KB) == 0
-            and kdim // KB <= n // PLANE * USED
+            and kdim <= 2 * PLANE * KB - KB
+            and kdim > 2 * PLANE * KB - 2 * KB
             and n1 == 512
             and n2 == 8 * n
         )

time: 45.9 us -> 43.1 us (0.939)
  Pallas kernels: 44.2 us -> 41.6 us
    pallas_call x1, Pallas kernels: 44.2 us -> 41.6 us  [fused(): pl.pallas_call(functools.partial(kernel, n), out_shape=jax.ShapeDtypeStru...]
    unnamed x1 -> x3, local copies, waits for them, and re-layouts: 1.53 us -> 1.3 us
where the time goes in v2:
time: 43.1 us; the launch traced here: 42.9 us
  Pallas kernels  41.6 us (97%)
  local copies, waits for them, and re-layouts  1.3 us (3%)
    pallas_call x1, Pallas kernels, fused(): pl.pallas_call(functools.partial(kernel, n), out_shape=jax.ShapeDtypeStru...  41.6 us
    unnamed x3, local copies, waits for them, and re-layouts  1.3 us

profile of v2, /device:TPU:0, one launch (start us, length us, event | category | flops | bytes accessed | tf_op | source)
XLA Modules:
  0.0 42.9 jit_solution(11009353923754260596)
XLA Ops:
  0.0 0.0 copy-start
  0.0 0.7 %copy-done = s32[2]{0:T(128)S(1)} copy-done((s32[2]{0:T(128)S(1)}, s32[2]{0:T(128)}, u32[]{:S(2)}) %copy-start) | copy-done | bytes 32
  0.7 41.6 %shard_map.46 = f32[176,128]{1,0:T(8,128)S(1)} custom-call(f32[352,512]{1,0:T(8,128)} %bitcast.7, f32[512,128]{1,0:T(8,128)} %sketch_one.1, f32[256,128]{1,0:T(8,128)} %sketch_two.1, s32[2]{0:T(128)S(1)} %copy-done), custom_call_target="tpu_custom_call" | custom-call | flops 600000000 | bytes 2000000 | tf_op jit(solution)/shard_map/pallas_call | solution.py:376
  42.3 0.6 %copy.6 = f32[4,44,128]{2,0,1:T(4,128)} copy(f32[4,44,128]{2,0,1:T(4,128)S(1)} %bitcast.6) | data formatting | bytes 180224
Async XLA Ops:
  0.0 0.7 %copy-start = (s32[2]{0:T(128)S(1)}, s32[2]{0:T(128)}, u32[]{:S(2)}) copy-start(s32[2]{0:T(128)} %ranks_in.1) | copy-start | bytes 28

commit v3 on v2

--- a/solution.py
+++ b/solution.py
@@ -36,11 +36,26 @@
     )
 
 
+def halves(x):
+    high = x.astype(jnp.bfloat16)
+    return high, (x - high.astype(jnp.float32)).astype(jnp.bfloat16)
+
+
+def mul(a, b, dims):
+    def one(x, y):
+        return lax.dot_general(
+            x, y, (dims, ((), ())), preferred_element_type=jnp.float32
+        )
+
+    (ah, al), (bh, bl) = halves(a), halves(b)
+    return one(ah, bh) + (one(ah, bl) + one(al, bh))
+
+
 NN = ((1,), (0,))
 NT = ((1,), (1,))
 TN = ((0,), (0,))
 BLOCK = 8
-TILES = 4
+TILES = 8
 KB = 3
 PLANE = 8
 
@@ -66,36 +81,36 @@
                     d[p, q] = jnp.broadcast_to(column[p : p + 1, :], tile)
                 for v in range(u + 1, TILES):
                     below[v, q] = jnp.broadcast_to(rows_a[v][:, lane : lane + 1], tile)
+            m = {}
             done_a, done_t = [], []
             panel_a = jnp.zeros(tile, jnp.float32)
             panel_t = jnp.zeros(tile, jnp.float32)
             for j in range(BLOCK):
                 x = d[j, j]
+                r = 1.0 / x
                 y = lax.rsqrt(x)
-                y = y * (1.5 - 0.5 * ((x * y) * y))
-                for p in range(j + 1, BLOCK):
-                    d[p, j] = d[p, j] * y
-                for v in range(u + 1, TILES):
-                    below[v, j] = below[v, j] * y
                 for q in range(j + 1, BLOCK):
                     for p in range(q, BLOCK):
-                        d[p, q] = d[p, q] - d[p, j] * d[q, j]
-                    for v in range(u + 1, TILES):
-                        below[v, q] = below[v, q] - below[v, j] * d[q, j]
+                        d[p, q] = d[p, q] - (d[p, j] * d[q, j]) * r
+                for p in range(j + 1, BLOCK):
+                    m[p, j] = d[p, j] * r
+                low = {}
+                for v in range(u + 1, TILES):
+                    low[v] = below[v, j] * r
+                    for q in range(j + 1, BLOCK):
+                        below[v, q] = below[v, q] - low[v] * d[q, j]
                 ra = jnp.broadcast_to(rows_a[u][j : j + 1, :], tile)
                 rt = jnp.broadcast_to(rows_t[u][j : j + 1, :], tile)
                 for k in range(j):
-                    ra = ra - d[j, k] * done_a[k]
-                    rt = rt - d[j, k] * done_t[k]
-                ra = ra * y
-                rt = rt * y
+                    ra = ra - m[j, k] * done_a[k]
+                    rt = rt - m[j, k] * done_t[k]
                 done_a.append(ra)
                 done_t.append(rt)
-                panel_a = jnp.where(sub == j, ra, panel_a)
-                panel_t = jnp.where(sub == j, rt, panel_t)
+                panel_a = jnp.where(sub == j, ra * y, panel_a)
+                panel_t = jnp.where(sub == j, rt * y, panel_t)
                 for v in range(u + 1, TILES):
-                    rows_a[v] = rows_a[v] - below[v, j] * ra
-                    rows_t[v] = rows_t[v] - below[v, j] * rt
+                    rows_a[v] = rows_a[v] - low[v] * ra
+                    rows_t[v] = rows_t[v] - low[v] * rt
             panels_a.append(panel_a)
             panels_t.append(panel_t)
         panel_t = jnp.concatenate(panels_t, axis=0)
@@ -220,15 +235,15 @@
     loads[1].wait()
     turned = s1[...].T * (sub < ranks[0]).astype(jnp.float32)
     loads[2].wait()
-    projected = dot(turned[:, :wide], flat[0, :lines, :], NT)
+    projected = mul(turned[:, :wide], flat[0, :lines, :], NT)
     loads[3].wait()
-    projected = projected + dot(turned[:, wide:], flat[1, :lines, :], NT)
-    part[1 - core] = dot(projected, flat[1 - core, pl.ds(0, lines), :], NN)
+    projected = projected + mul(turned[:, wide:], flat[1, :lines, :], NT)
+    part[1 - core] = mul(projected, flat[1 - core, pl.ds(0, lines), :], NN)
 
     pl.semaphore_wait(barrier, n - 1)
     copy(0, part.at[1 - core], pair, twin).start()
     later(0, pair)
-    part[core] = dot(projected, flat[core, pl.ds(0, lines), :], NN)
+    part[core] = mul(projected, flat[core, pl.ds(0, lines), :], NN)
     copy(0, pair, pair, twin).wait_recv()
     mine[...] = part[core] + pair[...]
     for i, (m, peer) in enumerate(alike):
@@ -247,7 +262,7 @@
     copy(3, full.at[core], full.at[core], twin).start()
     later(3, pair)
     sk = full[core]
-    rot[...] = dot(flat[core], sk, NT).reshape(rot.shape)
+    rot[...] = mul(flat[core], sk, NT).reshape(rot.shape)
     inner = dot(sk, sk, NT)
     copy(3, pair, pair, twin).wait_recv()
     sk = full[1 - core]
@@ -258,7 +273,7 @@
         first = base - PLANE
         ks = pl.ds(KB * first, KB * PLANE)
         span = pl.ds(pl.multiple_of(first * (KB * ydev), part_lines), part_lines)
-        more = dot(flat[1 - core, span, :], sk, NT)
+        more = mul(flat[1 - core, span, :], sk, NT)
         rot[ks] = rot[ks] + more.reshape(KB * PLANE, ydev, size)
         for b in inside:
             peer = b + base
@@ -289,14 +304,15 @@
     @pl.when(holds)
     def _():
         for k in range(KB):
-            stack[k * size : (k + 1) * size, :] = dot(linv[...], have[k], NT)
+            stack[k * size : (k + 1) * size, :] = mul(linv[...], have[k], NT)
         mixed = stack[...]
-        spread = dot(s2t, mixed, NT)
-        total = dot(spread, mixed, NN)
+        spread = mul(s2t, mixed, NT)
+        total = mul(spread, mixed, NN)
         part_two[...] = total
 
     def of_slot(j):
-        return pl.ds(pl.multiple_of(j * rows, rows), rows)
+        place = lax.rem(j, 2) * PLANE + j // 2
+        return pl.ds(pl.multiple_of(place * rows, rows), rows)
 
     @pl.when(holds)
     def _():
@@ -332,7 +348,7 @@
 
     @pl.when(holds)
     def _():
-        spun = dot(stack[...], full_two[...], NT)
+        spun = mul(stack[...], full_two[...], NT)
         for d in range(n):
             for k in range(KB):
                 give[d, k] = spun[k * size + per * d : k * size + per * (d + 1), :]
@@ -342,7 +358,7 @@
 
     later(8, give.at[pl.ds(0, n - 1)], holds)
     sk = full_two[...]
-    fill_work(work, dot(sk, sk, NT), keep_two, size)
+    fill_work(work, mul(sk, sk, NT), keep_two, size)
     inverse_factor(work, linv)
 
     @pl.when(holds)
@@ -354,7 +370,7 @@
     def _():
         copy(8, last, last, twin).wait_recv()
 
-    done = dot(last[...].reshape(holders * KB * per, size), linv[...], NT)
+    done = mul(last[...].reshape(holders * KB * per, size), linv[...], NT)
     out[...] = done[: out.shape[0], :]
 
     for wait in waits:
@@ -375,7 +391,7 @@
     lines = jnp.transpose(field, (1, 0, 2)).reshape(kdim * ydev, n1)
     core = pl.pallas_call(
         functools.partial(kernel, n),
-        out_shape=jax.ShapeDtypeStruct((kdim * per, size), f32),
+        out_shape=pltpu.VMEM((kdim * per, size), f32),
         in_specs=[hbm, hbm, hbm, hbm],
         out_specs=pl.BlockSpec(memory_space=pltpu.VMEM),
         scratch_shapes=[
@@ -403,7 +419,7 @@
             pltpu.SemaphoreType.DMA((9,)),
         ],
         compiler_params=pltpu.CompilerParams(
-            collective_id=0, has_side_effects=True, vmem_limit_bytes=55075 * 1024
+            collective_id=0, has_side_effects=True, vmem_limit_bytes=56 * 1024 * 1024
         ),
         cost_estimate=pl.CostEstimate(
             flops=600_000_000, bytes_accessed=2_000_000, transcendentals=256

time: 43.1 us -> 40.7 us (0.944)
  Pallas kernels: 41.6 us -> 39.9 us
  local copies, waits for them, and re-layouts: 1.3 us -> 0.64 us
    pallas_call x1, Pallas kernels: 41.6 us -> 39.9 us  [fused(): pl.pallas_call(functools.partial(kernel, n), out_shape=pltpu.VMEM((kdim *...]
    unnamed x3 -> x1, local copies, waits for them, and re-layouts: 1.3 us -> 0.64 us
where the time goes in v3:
time: 40.7 us; the launch traced here: 40.6 us
  Pallas kernels  39.9 us (98%)
  local copies, waits for them, and re-layouts  0.64 us (2%)
    pallas_call x1, Pallas kernels, fused(): pl.pallas_call(functools.partial(kernel, n), out_shape=pltpu.VMEM((kdim *...  39.9 us

profile of v3, /device:TPU:0, one launch (start us, length us, event | category | flops | bytes accessed | tf_op | source)
XLA Modules:
  0.0 40.6 jit_solution(8302609880448862486)
XLA Ops:
  0.0 39.9 %shard_map.46 = f32[176,128]{1,0:T(8,128)S(1)} custom-call(f32[352,512]{1,0:T(8,128)} %bitcast.7, f32[512,128]{1,0:T(8,128)} %sketch_one.1, f32[256,128]{1,0:T(8,128)} %sketch_two.1, s32[2]{0:T(128)} %ranks_in.1), custom_call_target="tpu_custom_call" | custom-call | flops 600000000 | bytes 2000000 | tf_op jit(solution)/shard_map/pallas_call | solution.py:392
  39.9 0.6 %copy.6 = f32[4,44,128]{2,0,1:T(4,128)} copy(f32[4,44,128]{2,0,1:T(4,128)S(1)} %bitcast.6) | data formatting | bytes 180224

commit v4 on v3

--- a/solution.py
+++ b/solution.py
@@ -72,15 +72,26 @@
         rows_a = [own[u * BLOCK : (u + 1) * BLOCK, :] for u in range(TILES)]
         rows_t = [rest[u * BLOCK : (u + 1) * BLOCK, :] for u in range(TILES)]
         panels_a, panels_t = [], []
+        ahead = None
         for u in range(TILES):
             d, below = {}, {}
             for q in range(BLOCK):
                 lane = r0 + u * BLOCK + q
-                column = jnp.broadcast_to(rows_a[u][:, lane : lane + 1], tile)
+                if ahead is None:
+                    column = jnp.broadcast_to(rows_a[u][:, lane : lane + 1], tile)
+                else:
+                    column = ahead[q]
                 for p in range(q, BLOCK):
                     d[p, q] = jnp.broadcast_to(column[p : p + 1, :], tile)
                 for v in range(u + 1, TILES):
                     below[v, q] = jnp.broadcast_to(rows_a[v][:, lane : lane + 1], tile)
+            ahead = None
+            if u + 1 < TILES:
+                first = r0 + (u + 1) * BLOCK
+                ahead = [
+                    jnp.broadcast_to(rows_a[u + 1][:, first + q : first + q + 1], tile)
+                    for q in range(BLOCK)
+                ]
             m = {}
             done_a, done_t = [], []
             panel_a = jnp.zeros(tile, jnp.float32)
@@ -97,6 +108,10 @@
                 low = {}
                 for v in range(u + 1, TILES):
                     low[v] = below[v, j] * r
+                    if v == u + 1:
+                        for q in range(BLOCK):
+                            across = jnp.broadcast_to(below[v, j][q : q + 1, :], tile)
+                            ahead[q] = ahead[q] - low[v] * across
                     for q in range(j + 1, BLOCK):
                         below[v, q] = below[v, q] - low[v] * d[q, j]
                 ra = jnp.broadcast_to(rows_a[u][j : j + 1, :], tile)

time: 40.7 us -> 39.8 us (0.978)
  Pallas kernels: 39.9 us -> 38.9 us
    pallas_call x1, Pallas kernels: 39.9 us -> 38.9 us  [fused(): pl.pallas_call(functools.partial(kernel, n), out_shape=pltpu.VMEM((kdim *...]
where the time goes in v4:
time: 39.8 us; the launch traced here: 39.6 us
  Pallas kernels  38.9 us (98%)
  local copies, waits for them, and re-layouts  0.64 us (2%)
    pallas_call x1, Pallas kernels, fused(): pl.pallas_call(functools.partial(kernel, n), out_shape=pltpu.VMEM((kdim *...  38.9 us

profile of v4, /device:TPU:0, one launch (start us, length us, event | category | flops | bytes accessed | tf_op | source)
XLA Modules:
  0.0 39.6 jit_solution(15433743961981636671)
XLA Ops:
  0.0 38.9 %shard_map.46 = f32[176,128]{1,0:T(8,128)S(1)} custom-call(f32[352,512]{1,0:T(8,128)} %bitcast.7, f32[512,128]{1,0:T(8,128)} %sketch_one.1, f32[256,128]{1,0:T(8,128)} %sketch_two.1, s32[2]{0:T(128)} %ranks_in.1), custom_call_target="tpu_custom_call" | custom-call | flops 600000000 | bytes 2000000 | tf_op jit(solution)/shard_map/pallas_call | solution.py:407
  39.0 0.6 %copy.6 = f32[4,44,128]{2,0,1:T(4,128)} copy(f32[4,44,128]{2,0,1:T(4,128)S(1)} %bitcast.6) | data formatting | bytes 180224

commit v5 on v4

--- a/solution.py
+++ b/solution.py
@@ -157,7 +157,7 @@
     n, field, sketch_one, sketch_two, ranks_in, out,
     flat, s1, s2, ranks, part, pair, mine, got, full, rot, have, work, linv, stack,
     part_two, got_two, full_two, give, last,
-    load_sem, send_sem, recv_sem,
+    load_sem, send_sem, recv_sem, note,
 ):
     me = lax.axis_index("wide")
     size = s1.shape[1]
@@ -191,11 +191,26 @@
     barrier = pltpu.get_barrier_semaphore()
 
     def greet(i, carry):
-        peer = lax.rem(me + 1 + i, n)
+        peer = 2 * lax.rem(chip + 1 + i, chips) + 1
         pl.semaphore_signal(barrier, inc=1, device_id={"wide": peer}, device_id_type=MESH)
         return carry
 
-    lax.fori_loop(0, n - 1, greet, 0)
+    lax.fori_loop(0, chips - 1, greet, 0)
+    leads = core == 1
+    follows = core == 0
+    twin = chip * 2 + 1 - core
+
+    def nod():
+        pl.semaphore_signal(note, inc=1, device_id={"wide": twin}, device_id_type=MESH)
+
+    @pl.when(leads)
+    def _():
+        pl.semaphore_signal(barrier, inc=1, device_id={"wide": twin}, device_id_type=MESH)
+
+    @pl.when(follows)
+    def _():
+        pl.semaphore_wait(barrier, 1)
+        nod()
 
     bits = n.bit_length() - 1
     deltas = [(1 - 2 * lax.rem(me // (1 << b), 2)) * (1 << b) for b in range(bits)]
@@ -204,7 +219,6 @@
         return me + sum(deltas[b] for b in range(bits) if (m >> b) & 1)
 
     alike = [(2 * m, flipped(2 * m)) for m in far_first(bits - 1, 2)]
-    twin = flipped(1)
 
     def copy(phase, source, target, peer):
         return pltpu.make_async_remote_copy(
@@ -255,12 +269,25 @@
     projected = projected + mul(turned[:, wide:], flat[1, :lines, :], NT)
     part[1 - core] = mul(projected, flat[1 - core, pl.ds(0, lines), :], NN)
 
-    pl.semaphore_wait(barrier, n - 1)
+    @pl.when(leads)
+    def _():
+        pl.semaphore_wait(note, 1)
+
     copy(0, part.at[1 - core], pair, twin).start()
     later(0, pair)
     part[core] = mul(projected, flat[core, pl.ds(0, lines), :], NN)
     copy(0, pair, pair, twin).wait_recv()
     mine[...] = part[core] + pair[...]
+
+    @pl.when(leads)
+    def _():
+        pl.semaphore_wait(barrier, n - 2)
+        nod()
+
+    @pl.when(follows)
+    def _():
+        pl.semaphore_wait(note, 1)
+
     for i, (m, peer) in enumerate(alike):
         copy(1, mine.at[of_chip(peer // 2), :], got.at[m // 2 - 1], peer).start()
     later(1, got)
@@ -432,6 +459,7 @@
             pltpu.SemaphoreType.DMA((5,)),
             pltpu.SemaphoreType.DMA((9,)),
             pltpu.SemaphoreType.DMA((9,)),
+            pltpu.SemaphoreType.REGULAR,
         ],
         compiler_params=pltpu.CompilerParams(
             collective_id=0, has_side_effects=True, vmem_limit_bytes=56 * 1024 * 1024

time: 39.8 us -> 38.4 us (0.965)
  Pallas kernels: 38.9 us -> 37.6 us
    pallas_call x1, Pallas kernels: 38.9 us -> 37.6 us  [fused(): pl.pallas_call(functools.partial(kernel, n), out_shape=pltpu.VMEM((kdim *...]
where the time goes in v5:
time: 38.4 us; the launch traced here: 38.3 us
  Pallas kernels  37.6 us (98%)
  local copies, waits for them, and re-layouts  0.64 us (2%)
    pallas_call x1, Pallas kernels, fused(): pl.pallas_call(functools.partial(kernel, n), out_shape=pltpu.VMEM((kdim *...  37.6 us

profile of v5, /device:TPU:0, one launch (start us, length us, event | category | flops | bytes accessed | tf_op | source)
XLA Modules:
  0.0 38.3 jit_solution(2511903991135137092)
XLA Ops:
  0.0 37.6 %shard_map.46 = f32[176,128]{1,0:T(8,128)S(1)} custom-call(f32[352,512]{1,0:T(8,128)} %bitcast.7, f32[512,128]{1,0:T(8,128)} %sketch_one.1, f32[256,128]{1,0:T(8,128)} %sketch_two.1, s32[2]{0:T(128)} %ranks_in.1), custom_call_target="tpu_custom_call" | custom-call | flops 600000000 | bytes 2000000 | tf_op jit(solution)/shard_map/pallas_call | solution.py:434
  37.6 0.6 %copy.6 = f32[4,44,128]{2,0,1:T(4,128)} copy(f32[4,44,128]{2,0,1:T(4,128)S(1)} %bitcast.6) | data formatting | bytes 180224

commit v6 on v5

--- a/solution.py
+++ b/solution.py
@@ -48,7 +48,16 @@
         )
 
     (ah, al), (bh, bl) = halves(a), halves(b)
-    return one(ah, bh) + (one(ah, bl) + one(al, bh))
+    rest = one(al, bh)
+    if dims == NT and b.shape[1] == 128:
+        joined = one(
+            jnp.concatenate([ah, ah], axis=1), jnp.concatenate([bh, bl], axis=1)
+        )
+        return joined + rest
+    if dims == NT and b.shape[0] == 128:
+        joined = one(ah, jnp.concatenate([bh, bl], axis=0))
+        return joined[:, :128] + (joined[:, 128:] + rest)
+    return one(ah, bh) + (one(ah, bl) + rest)
 
 
 NN = ((1,), (0,))
@@ -245,7 +254,7 @@
     slot = jnp.clip(me - PLANE, 0, 2 * PLANE - 1)
     holds = jnp.logical_and(middle, slot < holders)
     spare = jnp.logical_not(holds)
-    turns = (6, 7, 4, 5, 2, 3, 1, 0)
+    turns = (7, 6, 5, 4, 3, 2, 1, 0)
     inside = [below + sum(deltas[b] for b in range(3) if (m >> b) & 1) for m in turns]
     nearer = jnp.where(plane < 2, PLANE, 2 * PLANE)
     farther = 3 * PLANE - nearer
@@ -305,7 +314,7 @@
     later(3, pair)
     sk = full[core]
     rot[...] = mul(flat[core], sk, NT).reshape(rot.shape)
-    inner = dot(sk, sk, NT)
+    inner = mul(sk, sk, NT)
     copy(3, pair, pair, twin).wait_recv()
     sk = full[1 - core]
 
@@ -334,7 +343,7 @@
     def _():
         have[:, mine_y, :] = rot[pl.ds(KB * slot, KB)]
 
-    inner = inner + dot(sk, sk, NT)
+    inner = inner + mul(sk, sk, NT)
     fill_work(work, inner, keep_one, size)
     inverse_factor(work, linv)
 

time: 38.4 us -> 38.2 us (level)
  no operation moved by 1% of the time
where the time goes in v6:
time: 38.2 us; the launch traced here: 38 us
  Pallas kernels  37.4 us (98%)
  local copies, waits for them, and re-layouts  0.64 us (2%)
    pallas_call x1, Pallas kernels, fused(): pl.pallas_call(functools.partial(kernel, n), out_shape=pltpu.VMEM((kdim *...  37.4 us

profile of v6, /device:TPU:0, one launch (start us, length us, event | category | flops | bytes accessed | tf_op | source)
XLA Modules:
  0.0 38.0 jit_solution(15896313128332045279)
XLA Ops:
  0.0 37.4 %shard_map.46 = f32[176,128]{1,0:T(8,128)S(1)} custom-call(f32[352,512]{1,0:T(8,128)} %bitcast.7, f32[512,128]{1,0:T(8,128)} %sketch_one.1, f32[256,128]{1,0:T(8,128)} %sketch_two.1, s32[2]{0:T(128)} %ranks_in.1), custom_call_target="tpu_custom_call" | custom-call | flops 600000000 | bytes 2000000 | tf_op jit(solution)/shard_map/pallas_call | solution.py:443
  37.4 0.6 %copy.6 = f32[4,44,128]{2,0,1:T(4,128)} copy(f32[4,44,128]{2,0,1:T(4,128)S(1)} %bitcast.6) | data formatting | bytes 180224

commit v7 on v6

--- a/solution.py
+++ b/solution.py
@@ -318,7 +318,6 @@
     copy(3, pair, pair, twin).wait_recv()
     sk = full[1 - core]
 
-    mine_y = pl.ds(pl.multiple_of(me * ydev, ydev), ydev)
     part_lines = PLANE * KB * ydev
     for base in (farther, nearer):
         first = base - PLANE
@@ -333,7 +332,7 @@
             @pl.when(jnp.logical_and(j < holders, peer != me))
             def _():
                 copy(
-                    4, rot.at[pl.ds(KB * j, KB)], have.at[:, mine_y, :], peer
+                    4, rot.at[pl.ds(KB * j, KB)], have.at[me], peer
                 ).start()
 
     later(4, rot.at[pl.ds(0, KB * (holders - 1))], holds)
@@ -341,7 +340,7 @@
 
     @pl.when(holds)
     def _():
-        have[:, mine_y, :] = rot[pl.ds(KB * slot, KB)]
+        have[me] = rot[pl.ds(KB * slot, KB)]
 
     inner = inner + mul(sk, sk, NT)
     fill_work(work, inner, keep_one, size)
@@ -349,13 +348,15 @@
 
     @pl.when(holds)
     def _():
-        everything = have.at[:, pl.ds(0, n2 - ydev), :]
+        everything = have.at[pl.ds(0, n - 1)]
         copy(4, everything, everything, twin).wait_recv()
 
     @pl.when(holds)
     def _():
         for k in range(KB):
-            stack[k * size : (k + 1) * size, :] = mul(linv[...], have[k], NT)
+            stack[k * size : (k + 1) * size, :] = mul(
+                linv[...], have[:, k].reshape(n2, size), NT
+            )
         mixed = stack[...]
         spread = mul(s2t, mixed, NT)
         total = mul(spread, mixed, NN)
@@ -456,7 +457,7 @@
             pltpu.VMEM((chips - 1, rows, wide), f32),
             pltpu.VMEM((2, size, wide), f32),
             pltpu.VMEM((padded, ydev, size), f32),
-            pltpu.VMEM((KB, n2, size), f32),
+            pltpu.VMEM((n, KB, ydev, size), f32),
             pltpu.VMEM((size, 2 * size), f32),
             pltpu.VMEM((size, size), f32),
             pltpu.VMEM((KB * size, n2), f32),

time: 38.2 us -> 38.2 us (level)
  no operation moved by 1% of the time
where the time goes in v7:
time: 38.2 us; the launch traced here: 38 us
  Pallas kernels  37.4 us (98%)
  local copies, waits for them, and re-layouts  0.64 us (2%)
    pallas_call x1, Pallas kernels, fused(): pl.pallas_call(functools.partial(kernel, n), out_shape=pltpu.VMEM((kdim *...  37.4 us

profile of v7, /device:TPU:0, one launch (start us, length us, event | category | flops | bytes accessed | tf_op | source)
XLA Modules:
  0.0 38.0 jit_solution(15395547259844684512)
XLA Ops:
  0.0 37.4 %shard_map.46 = f32[176,128]{1,0:T(8,128)S(1)} custom-call(f32[352,512]{1,0:T(8,128)} %bitcast.7, f32[512,128]{1,0:T(8,128)} %sketch_one.1, f32[256,128]{1,0:T(8,128)} %sketch_two.1, s32[2]{0:T(128)} %ranks_in.1), custom_call_target="tpu_custom_call" | custom-call | flops 600000000 | bytes 2000000 | tf_op jit(solution)/shard_map/pallas_call | solution.py:444
  37.4 0.6 %copy.6 = f32[4,44,128]{2,0,1:T(4,128)} copy(f32[4,44,128]{2,0,1:T(4,128)S(1)} %bitcast.6) | data formatting | bytes 180224

commit v8 on v7

--- a/solution.py
+++ b/solution.py
@@ -101,40 +101,39 @@
                     jnp.broadcast_to(rows_a[u + 1][:, first + q : first + q + 1], tile)
                     for q in range(BLOCK)
                 ]
-            m = {}
             done_a, done_t = [], []
             panel_a = jnp.zeros(tile, jnp.float32)
             panel_t = jnp.zeros(tile, jnp.float32)
             for j in range(BLOCK):
-                x = d[j, j]
-                r = 1.0 / x
-                y = lax.rsqrt(x)
+                y = lax.rsqrt(d[j, j])
+                for p in range(j + 1, BLOCK):
+                    d[p, j] = d[p, j] * y
                 for q in range(j + 1, BLOCK):
                     for p in range(q, BLOCK):
-                        d[p, q] = d[p, q] - (d[p, j] * d[q, j]) * r
-                for p in range(j + 1, BLOCK):
-                    m[p, j] = d[p, j] * r
-                low = {}
+                        d[p, q] = d[p, q] - d[p, j] * d[q, j]
                 for v in range(u + 1, TILES):
-                    low[v] = below[v, j] * r
+                    low = below[v, j] * y
+                    below[v, j] = low
                     if v == u + 1:
                         for q in range(BLOCK):
-                            across = jnp.broadcast_to(below[v, j][q : q + 1, :], tile)
-                            ahead[q] = ahead[q] - low[v] * across
+                            across = jnp.broadcast_to(low[q : q + 1, :], tile)
+                            ahead[q] = ahead[q] - low * across
                     for q in range(j + 1, BLOCK):
-                        below[v, q] = below[v, q] - low[v] * d[q, j]
+                        below[v, q] = below[v, q] - low * d[q, j]
                 ra = jnp.broadcast_to(rows_a[u][j : j + 1, :], tile)
                 rt = jnp.broadcast_to(rows_t[u][j : j + 1, :], tile)
                 for k in range(j):
-                    ra = ra - m[j, k] * done_a[k]
-                    rt = rt - m[j, k] * done_t[k]
+                    ra = ra - d[j, k] * done_a[k]
+                    rt = rt - d[j, k] * done_t[k]
+                ra = ra * y
+                rt = rt * y
                 done_a.append(ra)
                 done_t.append(rt)
-                panel_a = jnp.where(sub == j, ra * y, panel_a)
-                panel_t = jnp.where(sub == j, rt * y, panel_t)
+                panel_a = jnp.where(sub == j, ra, panel_a)
+                panel_t = jnp.where(sub == j, rt, panel_t)
                 for v in range(u + 1, TILES):
-                    rows_a[v] = rows_a[v] - low[v] * ra
-                    rows_t[v] = rows_t[v] - low[v] * rt
+                    rows_a[v] = rows_a[v] - below[v, j] * ra
+                    rows_t[v] = rows_t[v] - below[v, j] * rt
             panels_a.append(panel_a)
             panels_t.append(panel_t)
         panel_t = jnp.concatenate(panels_t, axis=0)

time: 38.2 us -> 38.1 us (level)
  no operation moved by 1% of the time
where the time goes in v8:
time: 38.1 us; the launch traced here: 37.9 us
  Pallas kernels  37.3 us (98%)
  local copies, waits for them, and re-layouts  0.64 us (2%)
    pallas_call x1, Pallas kernels, fused(): pl.pallas_call(functools.partial(kernel, n), out_shape=pltpu.VMEM((kdim *...  37.3 us

profile of v8, /device:TPU:0, one launch (start us, length us, event | category | flops | bytes accessed | tf_op | source)
XLA Modules:
  0.0 37.9 jit_solution(10987556836453640102)
XLA Ops:
  0.0 37.3 %shard_map.46 = f32[176,128]{1,0:T(8,128)S(1)} custom-call(f32[352,512]{1,0:T(8,128)} %bitcast.7, f32[512,128]{1,0:T(8,128)} %sketch_one.1, f32[256,128]{1,0:T(8,128)} %sketch_two.1, s32[2]{0:T(128)} %ranks_in.1), custom_call_target="tpu_custom_call" | custom-call | flops 600000000 | bytes 2000000 | tf_op jit(solution)/shard_map/pallas_call | solution.py:443
  37.3 0.6 %copy.6 = f32[4,44,128]{2,0,1:T(4,128)} copy(f32[4,44,128]{2,0,1:T(4,128)S(1)} %bitcast.6) | data formatting | bytes 180224

commit v9 on v8

--- a/solution.py
+++ b/solution.py
@@ -64,7 +64,7 @@
 NT = ((1,), (1,))
 TN = ((0,), (0,))
 BLOCK = 8
-TILES = 8
+TILES = 4
 KB = 3
 PLANE = 8
 

time: 38.1 us -> 38.1 us (level)
  no operation moved by 1% of the time
where the time goes in v9:
time: 38.1 us; the launch traced here: 38 us
  Pallas kernels  37.3 us (98%)
  local copies, waits for them, and re-layouts  0.64 us (2%)
    pallas_call x1, Pallas kernels, fused(): pl.pallas_call(functools.partial(kernel, n), out_shape=pltpu.VMEM((kdim *...  37.3 us

profile of v9, /device:TPU:0, one launch (start us, length us, event | category | flops | bytes accessed | tf_op | source)
XLA Modules:
  0.0 38.0 jit_solution(12845753936639984417)
XLA Ops:
  0.0 37.3 %shard_map.46 = f32[176,128]{1,0:T(8,128)S(1)} custom-call(f32[352,512]{1,0:T(8,128)} %bitcast.7, f32[512,128]{1,0:T(8,128)} %sketch_one.1, f32[256,128]{1,0:T(8,128)} %sketch_two.1, s32[2]{0:T(128)} %ranks_in.1), custom_call_target="tpu_custom_call" | custom-call | flops 600000000 | bytes 2000000 | tf_op jit(solution)/shard_map/pallas_call | solution.py:443
  37.3 0.6 %copy.6 = f32[4,44,128]{2,0,1:T(4,128)} copy(f32[4,44,128]{2,0,1:T(4,128)S(1)} %bitcast.6) | data formatting | bytes 180224
